TPU v7x, 32 devices: a whole 2x2x4 slice. The times are simulated.
32 devices in a mesh: rows: 8 (over y, x, core), heads: 4 (over z).
Axes of the slice: x: 2, y: 2, z: 4, core: 2. Of those that a mesh axis runs over, the one named last changes fastest.
Arguments:
- token_ids: int32 [32, 1024], P('rows'), may hold values from 0 to 50271
- segment_ids: int32 [32, 1024], P('rows'), may hold values from 0 to 7, never falling along the last dimension, each value on 1 to 256 neighbouring positions
- row_fill: int32 [32], P('rows'), may hold values from 512 to 1024
- task_ids: int32 [32, 8], P('rows'), may hold values from 0 to 7
- labels: int32 [32, 8], P('rows'), may hold values from 0 to 2
- task_weights: int32 [8], replicated, may hold values from 1 to 4
- word_table: bfloat16 [50272, 1024], P('heads'), may hold values from -6 to 6
- position_table: bfloat16 [258, 1024], replicated, may hold values from -6 to 6
- norm_gains: float32 [3, 1024], replicated, may hold values from 0.5 to 1.5
- norm_biases: float32 [3, 1024], replicated, may hold values from -2 to 2
- dense_biases: float32 [4, 1024], replicated, may hold values from -2 to 2
- qkv_weight: bfloat16 [1024, 3072], replicated, may hold values from -0.1875 to 0.1875
- out_weight: bfloat16 [1024, 1024], replicated, may hold values from -0.5 to 0.5
- ffn_in: bfloat16 [1024, 4096], replicated, may hold values from -0.1875 to 0.1875
- ffn_bias: float32 [4096], replicated, may hold values from -2 to 2
- ffn_out: bfloat16 [4096, 1024], replicated, may hold values from -0.09375 to 0.09375
- vera_a: bfloat16 [1024, 1024], replicated, may hold values from -0.1875 to 0.1875
- vera_b: bfloat16 [1024, 1024], replicated, may hold values from -0.1875 to 0.1875
- scale_d: float32 [2, 1024], replicated, may hold values from 0.05 to 0.5
- scale_b: float32 [2, 1024], replicated, may hold values from -4 to 4
- task_heads: float32 [8, 3, 1024], replicated, may hold values from -0.1875 to 0.1875
- mom_d: float32 [2, 1024], replicated, may hold values from -0.75 to 0.75
- mom_b: float32 [2, 1024], replicated, may hold values from -0.75 to 0.75
- mom_heads: float32 [8, 3, 1024], replicated, may hold values from -4 to 4
- avg_d: float32 [2, 1024], replicated, may hold values from 0.05 to 0.5
- avg_b: float32 [2, 1024], replicated, may hold values from -4 to 4
- avg_heads: float32 [8, 3, 1024], replicated, may hold values from -0.1875 to 0.1875
Outputs:
- loss: float32 [], replicated
- new_mom_d: float32 [2, 1024], replicated
- new_mom_b: float32 [2, 1024], replicated
- new_mom_heads: float32 [8, 3, 1024], replicated
- new_d: float32 [2, 1024], replicated
- new_b: float32 [2, 1024], replicated
- new_heads: float32 [8, 3, 1024], replicated
- new_avg_d: float32 [2, 1024], replicated
- new_avg_b: float32 [2, 1024], replicated
- new_avg_heads: float32 [8, 3, 1024], replicated
- heads_low: bfloat16 [8, 3, 1024], replicated
- stats: float32 [2], replicated
Inputs may be any that keep to these rules, and one draw needn't show every extreme that they name: `segment_ids`: in each row segment numbers start at 0, never fall, take every value below 8 and no segment has more than 256 slots.
All inputs are finite; a program needn't handle non-finite values.
Results may differ from a plain program's by a relative error of at most 0.008.
Values may be sent and summed in bfloat16 or wider, within the bound.
A program may use at most 256 MiB of HBM per device.

v0:
```python
import jax
import jax.numpy as jnp
from jax import lax
from jax.sharding import PartitionSpec as P

HEADS = 16
HDIM = 64
TASKS = 8
CLASSES = 3


EPSILON = 1e-05
MOMENTUM = 0.9
AVERAGE = 0.8
RATE_D = 5.0
RATE_B = 20.0
RATE_HEADS = 0.3


def layer_norm(values, gain, shift):
    centred = values - jnp.mean(values, -1, keepdims=True)
    spread = jnp.mean(centred * centred, -1, keepdims=True)
    return centred * lax.rsqrt(spread + EPSILON) * gain + shift


def norm_back(values, gain, shift, grad):
    return jax.vjp(lambda inner: layer_norm(inner, gain, shift), values)[1](grad)[0]


def dot_right(left, right):
    return lax.dot_general(
        left, right, (((1,), (1,)), ((), ())), preferred_element_type=jnp.float32
    )


def dot_left(left, right):
    return lax.dot_general(
        left, right, (((0,), (0,)), ((), ())), preferred_element_type=jnp.float32
    )


def row_tables(seg_row, fill_row, task_row, label_row):
    slot = jnp.arange(seg_row.shape[0], dtype=jnp.int32)
    numbers = jnp.arange(task_row.shape[0], dtype=jnp.int32)
    starts = jnp.sum((seg_row[None, :] < numbers[:, None]).astype(jnp.int32), 1)
    member = (seg_row[:, None] == numbers[None, :]).astype(jnp.int32)
    first_slot = jnp.sum(member * starts[None, :], 1)
    position = 2 + slot - first_slot
    leading = ((slot == first_slot) & (slot < fill_row)).astype(jnp.int32)
    task = jnp.sum(member * task_row[None, :], 1)
    label = jnp.sum(member * label_row[None, :], 1)
    return (position, leading, task, label)


def row_mask(seg_row, fill_row):
    slot = jnp.arange(seg_row.shape[0], dtype=jnp.int32)
    same = seg_row[:, None] == seg_row[None, :]
    return same & ((slot[None, :] < fill_row) | (slot[:, None] == slot[None, :]))


def project(x_low, lat_q, lat_v, weight, adapter, bias_q, bias_v, gain_q, gain_v):
    count_rows = x_low.shape[0]
    proj = jnp.dot(x_low, weight, preferred_element_type=jnp.float32).reshape(
        count_rows, -1, 3, HDIM
    )
    extra_q = jnp.dot(lat_q, adapter, preferred_element_type=jnp.float32)
    extra_v = jnp.dot(lat_v, adapter, preferred_element_type=jnp.float32)
    query = proj[:, :, 0] + (bias_q + gain_q * extra_q).reshape(count_rows, -1, HDIM)
    value = proj[:, :, 2] + (bias_v + gain_v * extra_v).reshape(count_rows, -1, HDIM)
    joined = jnp.stack([query, proj[:, :, 1], value], 2)
    return joined.astype(jnp.bfloat16).reshape(count_rows, -1)


def row_scores(query, key, seg_row, fill_row):
    scores = jnp.einsum("qhe,khe->hqk", query, key, preferred_element_type=jnp.float32) * 0.125
    return jnp.where(row_mask(seg_row, fill_row)[None], scores, -1000000000.0)


def attend(packed):
    qkv, seg_row, fill_row = packed
    scores = row_scores(qkv[:, :, 0], qkv[:, :, 1], seg_row, fill_row)
    top = jnp.max(scores, -1, keepdims=True)
    expo = jnp.exp(scores - top)
    total = jnp.sum(expo, -1, keepdims=True)
    probs = (expo / total).astype(jnp.bfloat16)
    mixed = jnp.einsum("hqk,khe->qhe", probs, qkv[:, :, 2], preferred_element_type=jnp.float32)
    return (mixed.astype(jnp.bfloat16), (top + jnp.log(total))[..., 0])


def attend_back(packed):
    qkv, grad_out, log_total, seg_row, fill_row = packed
    key, value = (qkv[:, :, 1], qkv[:, :, 2])
    probs = jnp.exp(row_scores(qkv[:, :, 0], key, seg_row, fill_row) - log_total[..., None])
    grad_value = jnp.einsum(
        "hqk,qhe->khe", probs.astype(jnp.bfloat16), grad_out, preferred_element_type=jnp.float32
    )
    grad_probs = jnp.einsum("qhe,khe->hqk", grad_out, value, preferred_element_type=jnp.float32)
    grad_scores = probs * (grad_probs - jnp.sum(probs * grad_probs, -1, keepdims=True))
    grad_query = (
        jnp.einsum(
            "hqk,khe->qhe",
            grad_scores.astype(jnp.bfloat16),
            key,
            preferred_element_type=jnp.float32,
        )
        * 0.125
    )
    return jnp.stack([grad_query, grad_value], 2).astype(jnp.bfloat16)


def update(weight, grad, moment, average, rate):
    moment_new = MOMENTUM * moment + grad
    weight_new = weight - rate * (grad + MOMENTUM * moment_new)
    return (moment_new, weight_new, AVERAGE * average + (1.0 - AVERAGE) * weight_new)


def on_device(
    token_ids,
    segment_ids,
    row_fill,
    task_ids,
    labels,
    task_weights,
    word_table,
    position_table,
    norm_gains,
    norm_biases,
    dense_biases,
    qkv_weight,
    out_weight,
    ffn_in,
    ffn_bias,
    ffn_out,
    vera_a,
    vera_b,
    scale_d,
    scale_b,
    task_heads,
    mom_d,
    mom_b,
    mom_heads,
    avg_d,
    avg_b,
    avg_heads,
):
    groups = lax.axis_size("heads")
    my_index = lax.axis_index("heads")
    rows_dev, slots = token_ids.shape
    group_tokens = rows_dev * slots
    tok_dev = group_tokens // groups
    width_model = norm_gains.shape[1]
    rank_width = vera_a.shape[1]
    heads_dev = HEADS // groups
    tables = jax.vmap(row_tables)(segment_ids, row_fill, task_ids, labels)
    position, leading, task, label = [
        lax.dynamic_slice_in_dim(item.reshape(-1), my_index * tok_dev, tok_dev) for item in tables
    ]
    flat_ids = token_ids.reshape(-1)
    vocab_dev = word_table.shape[0]
    local_ids = flat_ids - my_index * vocab_dev
    inside = (local_ids >= 0) & (local_ids < vocab_dev)
    found = jnp.take(word_table, jnp.clip(local_ids, 0, vocab_dev - 1), axis=0).astype(jnp.float32)
    embedded = lax.psum_scatter(
        jnp.where(inside[:, None], found, 0.0).astype(jnp.bfloat16),
        "heads",
        scatter_dimension=0,
        tiled=True,
    ).astype(jnp.float32)
    embedded = embedded + jnp.take(position_table, position, axis=0).astype(jnp.float32)
    x_zero = layer_norm(embedded, norm_gains[0], norm_biases[0])
    x_low = x_zero.astype(jnp.bfloat16)
    latent = jnp.dot(x_low, vera_a, preferred_element_type=jnp.float32)
    lat_q = (latent * scale_d[0]).astype(jnp.bfloat16)
    lat_v = (latent * scale_d[1]).astype(jnp.bfloat16)
    columns = heads_dev * 3 * HDIM
    features = heads_dev * HDIM
    w_mine = lax.dynamic_slice_in_dim(qkv_weight, my_index * columns, columns, 1)
    adapter_mine = lax.dynamic_slice_in_dim(vera_b, my_index * features, features, 1)
    own = [
        lax.dynamic_slice_in_dim(item, my_index * features, features)
        for item in (dense_biases[0], dense_biases[1], scale_b[0], scale_b[1])
    ]
    packed_in = jnp.concatenate([x_low, lat_q, lat_v], 1)
    pieces = lax.all_gather(packed_in, "heads", axis=0, tiled=True)
    qkv_local = project(
        pieces[:, :width_model],
        pieces[:, width_model : width_model + rank_width],
        pieces[:, width_model + rank_width :],
        w_mine,
        adapter_mine,
        own[0],
        own[1],
        own[2],
        own[3],
    )
    qkv_rows = qkv_local.reshape(rows_dev, slots, heads_dev, 3, HDIM)
    mixed_rows, log_total = lax.map(attend, (qkv_rows, segment_ids, row_fill))
    mixed = lax.all_to_all(
        mixed_rows.reshape(group_tokens, heads_dev * HDIM),
        "heads",
        split_axis=0,
        concat_axis=1,
        tiled=True,
    )
    r_one = (
        x_zero + jnp.dot(mixed, out_weight, preferred_element_type=jnp.float32) + dense_biases[2]
    )
    x_one = layer_norm(r_one, norm_gains[1], norm_biases[1])
    hidden = (
        jnp.dot(x_one.astype(jnp.bfloat16), ffn_in, preferred_element_type=jnp.float32) + ffn_bias
    )
    active, gelu_pull = jax.vjp(lambda inner: jax.nn.gelu(inner, approximate=False), hidden)
    r_two = (
        x_one
        + jnp.dot(active.astype(jnp.bfloat16), ffn_out, preferred_element_type=jnp.float32)
        + dense_biases[3]
    )
    x_two = layer_norm(r_two, norm_gains[2], norm_biases[2])
    pick = (task[:, None] == jnp.arange(TASKS, dtype=jnp.int32)[None, :]).astype(jnp.float32)
    counts = lax.psum(jnp.sum(pick * leading[:, None].astype(jnp.float32), 0), ("rows", "heads"))
    coef = task_weights.astype(jnp.float32) / jnp.maximum(counts, 1.0)
    heads_table = task_heads.astype(jnp.bfloat16).reshape(TASKS * CLASSES, width_model)
    x_two_low = x_two.astype(jnp.bfloat16)
    logits = dot_right(x_two_low, heads_table).reshape(tok_dev, TASKS, CLASSES)
    chosen = jnp.sum(pick[:, :, None] * logits, 1)
    target = (label[:, None] == jnp.arange(CLASSES, dtype=jnp.int32)[None, :]).astype(jnp.float32)
    weight = leading.astype(jnp.float32) * jnp.sum(pick * coef[None, :], 1)
    loss_part = jnp.sum(weight * (jax.nn.logsumexp(chosen, -1) - jnp.sum(target * chosen, -1)))
    grad_chosen = weight[:, None] * (jax.nn.softmax(chosen, -1) - target)
    grad_logits = (
        (pick[:, :, None] * grad_chosen[:, None, :])
        .reshape(tok_dev, TASKS * CLASSES)
        .astype(jnp.bfloat16)
    )
    grad_heads = dot_left(grad_logits, x_two_low).reshape(TASKS, CLASSES, width_model)
    grad_two = jnp.dot(grad_logits, heads_table, preferred_element_type=jnp.float32)
    grad_r_two = norm_back(r_two, norm_gains[2], norm_biases[2], grad_two)
    grad_active = dot_right(grad_r_two.astype(jnp.bfloat16), ffn_out)
    grad_hidden = gelu_pull(grad_active)[0].astype(jnp.bfloat16)
    grad_one = grad_r_two + dot_right(grad_hidden, ffn_in)
    grad_r_one = norm_back(r_one, norm_gains[1], norm_biases[1], grad_one)
    grad_mixed = dot_right(grad_r_one.astype(jnp.bfloat16), out_weight).astype(jnp.bfloat16)
    grad_rows = lax.all_to_all(
        grad_mixed, "heads", split_axis=1, concat_axis=0, tiled=True
    ).reshape(rows_dev, slots, heads_dev, HDIM)
    grad_qv = lax.map(attend_back, (qkv_rows, grad_rows, log_total, segment_ids, row_fill))
    grad_tokens = lax.all_to_all(
        grad_qv.reshape(group_tokens, heads_dev * 2 * HDIM),
        "heads",
        split_axis=0,
        concat_axis=1,
        tiled=True,
    )
    grad_tokens = grad_tokens.reshape(tok_dev, HEADS, 2, HDIM)
    grad_query = grad_tokens[:, :, 0].reshape(tok_dev, width_model)
    grad_value = grad_tokens[:, :, 1].reshape(tok_dev, width_model)
    extra_q = jnp.dot(lat_q, vera_b, preferred_element_type=jnp.float32)
    extra_v = jnp.dot(lat_v, vera_b, preferred_element_type=jnp.float32)
    grad_b = jnp.stack(
        [
            jnp.sum(grad_query.astype(jnp.float32) * extra_q, 0),
            jnp.sum(grad_value.astype(jnp.float32) * extra_v, 0),
        ]
    )
    back_q = dot_right((grad_query.astype(jnp.float32) * scale_b[0]).astype(jnp.bfloat16), vera_b)
    back_v = dot_right((grad_value.astype(jnp.float32) * scale_b[1]).astype(jnp.bfloat16), vera_b)
    grad_d = jnp.stack([jnp.sum(latent * back_q, 0), jnp.sum(latent * back_v, 0)])
    grad_d, grad_b, grad_heads, loss = lax.psum(
        (grad_d, grad_b, grad_heads, loss_part), ("rows", "heads")
    )
    m_d, w_d, a_d = update(scale_d, grad_d, mom_d, avg_d, RATE_D)
    m_b, w_b, a_b = update(scale_b, grad_b, mom_b, avg_b, RATE_B)
    m_h, w_h, a_h = update(task_heads, grad_heads, mom_heads, avg_heads, RATE_HEADS)
    stats = jnp.stack([jnp.sqrt(jnp.mean(w_d * w_d)), jnp.sqrt(jnp.mean(w_b * w_b))])
    return (loss, m_d, m_b, m_h, w_d, w_b, w_h, a_d, a_b, a_h, w_h.astype(jnp.bfloat16), stats)


def solution(mesh):
    return jax.shard_map(
        on_device,
        mesh=mesh,
        in_specs=(
            P("rows", None),
            P("rows", None),
            P("rows"),
            P("rows", None),
            P("rows", None),
            P(),
            P("heads", None),
            P(),
            P(),
            P(),
            P(),
            P(),
            P(),
            P(),
            P(),
            P(),
            P(),
            P(),
            P(),
            P(),
            P(),
            P(),
            P(),
            P(),
            P(),
            P(),
            P(),
        ),
        out_specs=(P(), P(), P(), P(), P(), P(), P(), P(), P(), P(), P(), P()),
        check_vma=False,
    )
```

profile of v0, /device:TPU:0, one launch (start us, length us, event | category | flops | bytes accessed | tf_op | source)
XLA Modules:
  0.0 1507.1 jit_solution(14750187530651141431)
XLA Ops:
  8.9 32.5 %gather_fusion = bf16[4096,1024]{1,0:T(8,128)(2,1)} fusion(bf16[12568,1024]{1,0:T(8,128)(2,1)} %param.37, s32[4096]{0:T(1024)S(1)} %broadcast_clamp_fusion), kind=kCustom, calls=%fused_computation | custom fusion | bytes 16793600 | tf_op jit(solution)/shard_map/jit(_take)/gather | solution.py:162
  41.4 7.9 select_convert_fusion
  58.7 137.9 %reduce-scatter.2.cloned.1.call-done = bf16[1024,1024]{1,0:T(8,128)(2,1)} async-done(((bf16[4096,1024]{1,0:T(8,128)(2,1)}), bf16[1024,1024]{1,0:T(8,128)(2,1)}) %reduce-scatter.2.cloned.1.call-update) | async-done | bytes 2097168 | tf_op jit(solution)/shard_map/reduce_scatter | solution.py:163
  214.2 424.7 %all-gather.2.cloned.1.call-done = bf16[4096,3072]{1,0:T(8,128)(2,1)} async-done(((bf16[1024,3072]{1,0:T(8,128)(2,1)}), bf16[4096,3072]{1,0:T(8,128)(2,1)}) %all-gather.2.cloned.1.call-update) | async-done | bytes 25165840 | tf_op jit(solution)/shard_map/all_gather | solution.py:184
  638.9 10.1 fusion.44
  675.1 7.4 pad_maximum_fusion.2
  687.4 68.9 %while.22 = (s32[]{:T(128)}, bf16[4,1024,4,64]{1,3,2,0:T(8,128)(2,1)}, f32[4,4,1024]{2,1,0:T(4,128)}, bf16[4,1024,4,3,64]{1,4,2,3,0:T(8,128)(2,1)}, s32[4,1024]{1,0:T(4,128)S(1)}, /*index=5*/s32[4]{0:T(128)S(1)}, s32[]{:T(128)}) while((s32[]{:T(128)}, bf16[4,1024,4,64]{1,3,2,0:T(8,128)(2,1)}, f32[4,4,1024]{2,1,0:T(4,128)}, ...), condition=%wide.region_12.13_spmd, body=%wide.region_9.12_spmd.sunk | while | flops 1128526848 | bytes 59915364 | solution.py:197
  761.8 68.1 %psum.35 = f32[8]{0:T(128)S(1)} all-reduce(f32[8]{0:T(128)S(1)} %select_reduce_fusion.4), channel_id=1, replica_groups=mesh['rows'=8,'heads'=4] {'rows','heads'}, use_global_device_ids=true, to_apply=%region_4.5 | all-reduce | flops 8 | bytes 64 | tf_op jit(solution)/shard_map/psum | solution.py:220
  839.5 47.9 %fusion.33 = (f32[1024,4096]{1,0:T(8,128)}, f32[1024,4096]{1,0:T(8,128)}) fusion(f32[4096]{0:T(1024)S(1)} %copy-done.76, bf16[1024,4096]{1,0:T(8,128)(2,1)S(1)} %bitcast.268, f32[1024,1024]{1,0:T(8,128)S(1)} %get-tuple-element.189, f32[1024]{0:T(1024)S(1)} %bitcast.253, f32[1024]{0:T(1024)S(1)} %bitcast.250, f32[1024]{0:T(1024)S(1)} %fusion.95, ...), kind=kOutput, calls=%fused_computation.56 | convolution fusion | flops 8859418624 | bytes 46170112 | tf_op jit(solution)/shard_map/dot_general | solution.py:210
  887.4 24.9 %fusion.116 = (f32[1024]{0:T(1024)S(1)}, f32[1024,1024]{1,0:T(8,128)}) fusion(f32[1024]{0:T(1024)S(1)} %bitcast.261, bf16[4096,1024]{1,0:T(8,128)(2,1)} %param.46, f32[1024,4096]{1,0:T(8,128)} %get-tuple-element.190, f32[1024,4096]{1,0:T(8,128)} %get-tuple-element.191, f32[4096]{0:T(1024)S(1)} %copy-done.76, f32[1024]{0:T(1024)S(1)} %bitcast.254, ...), kind=kOutput, calls=%fused_computation.240 | convolution fusion | flops 8614050816 | bytes 50372608 | tf_op jit(solution)/shard_map/dot_general | solution.py:215
  925.2 24.0 %add_convert_fusion.6.clone.4 = bf16[1024,4096]{1,0:T(8,128)(2,1)} fusion(f32[1024,4096]{1,0:T(8,128)} %get-tuple-element.190, f32[1024,4096]{1,0:T(8,128)} %get-tuple-element.191, f32[4096]{0:T(1024)S(1)} %copy-done.76, bf16[4096,1024]{1,0:T(8,128)(2,1)} %param.46, f32[1024,1024]{1,0:T(8,128)} %get-tuple-element.158, ...), kind=kOutput, calls=%fused_computation.57.clone.clone.clone.clone.clone.clone.1 | convolution fusion | flops 8654946304 | bytes 54546432 | tf_op jit(solution)/shard_map/dot_general | solution.py:31
  949.3 16.4 %multiply_reduce_fusion.5 = (f32[1024]{0:T(1024)S(1)}, f32[1024,1024]{1,0:T(8,128)S(1)}) fusion(f32[1024,1024]{1,0:T(8,128)} %copy-done.8, f32[1024]{0:T(1024)S(1)} %broadcast_multiply_fusion.1, f32[1024]{0:T(1024)S(1)} %bitcast.252, bf16[1024,4096]{1,0:T(8,128)(2,1)} %param.44, f32[1024,1024]{1,0:T(8,128)} %get-tuple-element.158, ...), kind=kOutput, calls=%fused_computation.104 | convolution fusion | flops 8596225024 | bytes 29376512 | tf_op jit(solution)/shard_map/dot_general | solution.py:31
  975.9 47.7 %all-to-all-done.1 = bf16[1024,4,256]{0,2,1:T(8,128)(2,1)} async-done(((bf16[1024,4,256]{0,2,1:T(8,128)(2,1)}), bf16[1024,4,256]{0,2,1:T(8,128)(2,1)}, u32[]{:S(2)}, u32[]{:S(2)}) %all-to-all-start.1) | async-done | bytes 2097184 | tf_op jit(solution)/shard_map/all_to_all | solution.py:243
  1023.6 199.1 %while.23 = (s32[]{:T(128)}, bf16[4,1024,4,2,64]{1,4,3,2,0:T(8,128)(2,1)}, bf16[4,1024,4,3,64]{1,4,2,3,0:T(8,128)(2,1)}, s32[4,1024]{1,0:T(4,128)}, s32[4]{0:T(1...) while((s32[]{:T(128)}, bf16[4,1024,4,2,64]{1,4,3,2,0:T(8,128)(2,1)}, ...), condition=%wide.region_31.32_spmd, body=%wide.region_29.31_spmd.sunk | while | flops 2190734336 | bytes 112295536 | solution.py:246
  1025.1 9.1 fusion.157
  1038.4 12.7 multiply_reduce_fusion.14
  1051.1 12.6 fusion.160
  1063.7 8.6 fusion.159
  1074.9 9.1 fusion.157
  1088.2 12.7 multiply_reduce_fusion.14
  1100.9 12.6 fusion.160
  1113.5 8.6 fusion.159
  1124.6 9.1 fusion.157
  1138.0 12.7 multiply_reduce_fusion.14
  1150.6 12.6 fusion.160
  1163.2 8.6 fusion.159
  1174.4 9.1 fusion.157
  1187.7 12.7 multiply_reduce_fusion.14
  1200.4 12.6 fusion.160
  1213.0 8.6 fusion.159
  1229.0 185.1 %all-reduce.3.cloned.1.call-done = f32[8,3,1024]{2,0,1:T(8,128)} async-done(((f32[8,3,1024]{2,0,1:T(8,128)}), f32[8,3,1024]{2,0,1:T(8,128)}) %all-reduce.3.cloned.1.call-update) | async-done | bytes 98320 | tf_op jit(solution)/shard_map/psum | solution.py:268
  1452.8 41.6 %all-reduce = (f32[]{:T(128)}, f32[2,1024]{1,0:T(2,128)S(1)}, f32[2,1024]{1,0:T(2,128)S(1)}) all-reduce(f32[]{:T(128)} %get-tuple-element.159, f32[2,1024]{1,0:T(2,128)S(1)} %pad_maximum_fusion.3, f32[2,1024]{1,0:T(2,128)S(1)} %pad_maximum_fusion.4), channel_id=1, replica_groups=mesh['rows'=8,'heads'=4] {'rows','heads'}, use_global_device_ids=true, to_apply=%region_23.24 | all-reduce | flops 4097 | bytes 32776 | tf_op jit(solution)/shard_map/psum | solution.py:268
  (337 shorter events, 241.9 us)
Async XLA Ops:
  7.2 196.1 %copy-start = (bf16[1024,1024]{1,0:T(8,128)(2,1)S(1)}, bf16[1024,1024]{1,0:T(8,128)(2,1)}, u32[]{:S(2)}) copy-start(bf16[1024,1024]{1,0:T(8,128)(2,1)} %param.47) | copy-start | bytes 6291460
  7.2 189.5 %reduce-scatter.2.cloned.1.call-start = ((), (), s32[]{:S(2)}) async-start(), calls=%async_computation.4 | async-start | bytes 10485760 | tf_op jit(solution)/shard_map/reduce_scatter | solution.py:163
  49.4 589.5 %all-gather.2.cloned.1.call-start = ((), (), s32[]{:S(2)}) async-start(), calls=%async_computation.5 | async-start | bytes 31457280 | tf_op jit(solution)/shard_map/all_gather | solution.py:184
  57.5 144.2 %copy-start.54 = (pred[1024]{0:T(1024)(128)(4,1)}, pred[1024]{0:T(1024)(128)(4,1)S(1)}, u32[]{:S(2)}) copy-start(pred[1024]{0:T(1024)(128)(4,1)S(1)} %compare_and_fusion.1) | copy-start | bytes 3076
  58.1 143.6 %copy-start.50 = (f32[1,1024]{1,0:T(1,128)}, f32[1,1024]{1,0:T(1,128)S(1)}, u32[]{:S(2)}) copy-start(f32[1,1024]{1,0:T(1,128)S(1)} %get-tuple-element.172) | copy-start | bytes 12292
  58.7 143.0 %copy-start.52 = (f32[1,1024]{1,0:T(1,128)}, f32[1,1024]{1,0:T(1,128)S(1)}, u32[]{:S(2)}) copy-start(f32[1,1024]{1,0:T(1,128)S(1)} %get-tuple-element.175) | copy-start | bytes 12292
  214.1 434.9 %copy-start.62 = (f32[1,1024]{1,0:T(1,128)}, f32[1,1024]{1,0:T(1,128)S(1)}, u32[]{:S(2)}) copy-start(f32[1,1024]{1,0:T(1,128)S(1)} %get-tuple-element.184) | copy-start | bytes 12292
  214.1 434.9 %copy-start.64 = (f32[1,1024]{1,0:T(1,128)}, f32[1,1024]{1,0:T(1,128)S(1)}, u32[]{:S(2)}) copy-start(f32[1,1024]{1,0:T(1,128)S(1)} %get-tuple-element.183) | copy-start | bytes 12292
  756.2 73.6 %copy-start.31 = (s32[4,1024]{1,0:T(4,128)S(1)}, s32[4,1024]{1,0:T(4,128)}, u32[]{:S(2)}) copy-start(s32[4,1024]{1,0:T(4,128)} %get-tuple-element.114) | copy-start | bytes 49156
  756.2 74.2 %copy-start.77 = (s32[8]{0:T(128)S(1)}, s32[8]{0:T(128)}, u32[]{:S(2)}) copy-start(s32[8]{0:T(128)} %param.36) | copy-start | bytes 100
  756.2 75.5 %copy-start.6 = (bf16[1024,1024]{1,0:T(8,128)(2,1)S(1)}, bf16[1024,1024]{1,0:T(8,128)(2,1)}, u32[]{:S(2)}) copy-start(bf16[1024,1024]{1,0:T(8,128)(2,1)} %gather_fusion.1) | copy-start | bytes 6291460
  756.3 75.5 %copy-start.36 = (f32[1024]{0:T(1024)S(1)}, f32[1024]{0:T(1024)}, u32[]{:S(2)}) copy-start(f32[1024]{0:T(1024)} %copy-done.35) | copy-start | bytes 12292
  756.3 75.5 %copy-start.49 = (f32[1024]{0:T(1024)S(1)}, f32[1024]{0:T(1024)}, u32[]{:S(2)}) copy-start(f32[1024]{0:T(1024)} %copy-done.48) | copy-start | bytes 12292
  756.3 75.5 %copy-start.51 = (f32[1,1024]{1,0:T(1,128)S(1)}, f32[1,1024]{1,0:T(1,128)}, u32[]{:S(2)}) copy-start(f32[1,1024]{1,0:T(1,128)} %copy-done.50) | copy-start | bytes 12292
  756.3 75.5 %copy-start.53 = (f32[1,1024]{1,0:T(1,128)S(1)}, f32[1,1024]{1,0:T(1,128)}, u32[]{:S(2)}) copy-start(f32[1,1024]{1,0:T(1,128)} %copy-done.52) | copy-start | bytes 12292
  756.3 75.5 %copy-start.55 = (pred[1024]{0:T(1024)(128)(4,1)S(1)}, pred[1024]{0:T(1024)(128)(4,1)}, u32[]{:S(2)}) copy-start(pred[1024]{0:T(1024)(128)(4,1)} %copy-done.54) | copy-start | bytes 3076
  756.3 75.5 %copy-start.69 = (f32[1,1024]{1,0:T(1,128)S(1)}, f32[1,1024]{1,0:T(1,128)}, u32[]{:S(2)}) copy-start(f32[1,1024]{1,0:T(1,128)} %get-tuple-element.180) | copy-start | bytes 12292
  756.3 75.4 %all-to-all-start = ((bf16[4,1024,256]{1,2,0:T(8,128)(2,1)}), bf16[4,1024,256]{1,2,0:T(8,128)(2,1)}, u32[]{:S(2)}, u32[]{:S(2)}) async-start(bf16[4,1024,256]{1,2,0:T(8,128)(2,1)} %bitcast.33), calls=%async_computation.1 | async-start | bytes 4194304 | tf_op jit(solution)/shard_map/all_to_all | solution.py:198
  838.6 48.7 %copy-start.8 = (f32[1024,1024]{1,0:T(8,128)}, f32[1024,1024]{1,0:T(8,128)S(1)}, u32[]{:S(2)}) copy-start(f32[1024,1024]{1,0:T(8,128)S(1)} %get-tuple-element.189) | copy-start | bytes 12582916
  839.3 48.1 %copy-start.37 = (f32[1024]{0:T(1024)}, f32[1024]{0:T(1024)S(1)}, u32[]{:S(2)}) copy-start(f32[1024]{0:T(1024)S(1)} %multiply_reduce_fusion.8) | copy-start | bytes 12292
  839.5 47.9 %copy-start.68 = (f32[1,1024]{1,0:T(1,128)S(1)}, f32[1,1024]{1,0:T(1,128)}, u32[]{:S(2)}) copy-start(f32[1,1024]{1,0:T(1,128)} %get-tuple-element.177) | copy-start | bytes 12292
  971.0 52.5 %copy-start.73 = (s32[4]{0:T(128)S(1)}, s32[4]{0:T(128)}, u32[]{:S(2)}) copy-start(s32[4]{0:T(128)} %param.33) | copy-start | bytes 52
  971.0 52.5 %all-to-all-start.1 = ((bf16[1024,4,256]{0,2,1:T(8,128)(2,1)}), bf16[1024,4,256]{0,2,1:T(8,128)(2,1)}, u32[]{:S(2)}, u32[]{:S(2)}) async-start(bf16[1024,4,256]{0,2,1:T(8,128)(2,1)} %bitcast.44), calls=%async_computation.2 | async-start | bytes 4194304 | tf_op jit(solution)/shard_map/all_to_all | solution.py:243
  1222.7 191.5 %copy-start.19 = (f32[8,3,1024]{2,0,1:T(8,128)S(1)}, f32[8,3,1024]{2,0,1:T(8,128)}, u32[]{:S(2)}) copy-start(f32[8,3,1024]{2,0,1:T(8,128)} %param.51) | copy-start | bytes 294916
  1222.7 191.5 %copy-start.29 = (f32[8,3,1024]{2,0,1:T(8,128)S(1)}, f32[8,3,1024]{2,0,1:T(8,128)}, u32[]{:S(2)}) copy-start(f32[8,3,1024]{2,0,1:T(8,128)} %param.54) | copy-start | bytes 294916
  1222.7 193.0 %copy-start.28 = (f32[8,3,1024]{2,0,1:T(8,128)S(1)}, f32[8,3,1024]{2,0,1:T(8,128)}, u32[]{:S(2)}) copy-start(f32[8,3,1024]{2,0,1:T(8,128)} %param.57) | copy-start | bytes 294916
  1222.7 193.7 %all-to-all-start.2 = ((bf16[4,1024,512]{1,2,0:T(8,128)(2,1)}), bf16[4,1024,512]{1,2,0:T(8,128)(2,1)}, u32[]{:S(2)}, u32[]{:S(2)}) async-start(bf16[4,1024,512]{1,2,0:T(8,128)(2,1)} %bitcast.47), calls=%async_computation.3 | async-start | bytes 8388608 | tf_op jit(solution)/shard_map/all_to_all | solution.py:247
  1227.7 186.4 %all-reduce.3.cloned.1.call-start = ((), (), s32[]{:S(2)}) async-start(), calls=%async_computation.6 | async-start | bytes 196608 | tf_op jit(solution)/shard_map/psum | solution.py:268
  1450.0 46.3 %copy-start.44 = (f32[2,1024]{1,0:T(2,128)S(1)}, f32[2,1024]{1,0:T(2,128)}, u32[]{:S(2)}) copy-start(f32[2,1024]{1,0:T(2,128)} %param.50) | copy-start | bytes 24580
  1450.0 48.8 %copy-start.58 = (f32[2,1024]{1,0:T(2,128)S(1)}, f32[2,1024]{1,0:T(2,128)}, u32[]{:S(2)}) copy-start(f32[2,1024]{1,0:T(2,128)} %param.56) | copy-start | bytes 24580
  1450.1 49.4 %copy-start.59 = (f32[2,1024]{1,0:T(2,128)S(1)}, f32[2,1024]{1,0:T(2,128)}, u32[]{:S(2)}) copy-start(f32[2,1024]{1,0:T(2,128)} %param.55) | copy-start | bytes 24580
  1450.1 50.0 %copy-start.1 = (bf16[1024,1024]{1,0:T(8,128)(2,1)S(1)}, bf16[1024,1024]{1,0:T(8,128)(2,1)}, u32[]{:S(2)}) copy-start(bf16[1024,1024]{1,0:T(8,128)(2,1)} %param.47) | copy-start | bytes 6291460
  (55 other events, 334.8 us)
Sparse Core Ops, SparseCore 0:
  49.5 147.1 reduce-scatter.1
  212.9 425.9 all-gather.1
  1234.7 179.3 all-reduce.2
where the time goes:
time: 1510 us
  waiting for transfers between devices  796 us (53%)
  matrix products  377 us (25%)
  blocking collectives  110 us (7%)
  local copies, waits for them, and re-layouts  103 us (7%)
  other arithmetic  90.1 us (6%)
  between operations  16.8 us (1%)
    all_gather x1, waiting for transfers between devices, on_device(): pieces = lax.all_gather(packed_in, 'heads', axis=0, tiled=True)  425 us
    psum x1, waiting for transfers between devices, on_device(): lax.psum((grad_d, grad_b, grad_heads, loss_part), ('rows', 'heads'))  185 us
    reduce_scatter x1, waiting for transfers between devices, on_device(): lax.psum_scatter(jnp.where(inside[:, None], found, 0.0).astype(jnp.bfloat...  138 us
    psum x1, blocking collectives, on_device(): lax.psum(jnp.sum(pick * leading[:, None].astype(jnp.float32), 0), ('rows'...  68.1 us
    dot_general x8, matrix products, row_scores(): jnp.einsum('qhe,khe->hqk', query, key, preferred_element_type=jnp.float32)  62.8 us
    dot_general x6, matrix products, dot_right(): lax.dot_general(left, right, (((1,), (1,)), ((), ())), preferred_element_...  50.3 us
    dot_general x4, matrix products, attend_back(): jnp.einsum('hqk,khe->qhe', grad_scores.astype(jnp.bfloat16), key, preferr...  50.3 us
    dot_general x1, matrix products, on_device(): jnp.dot(x_one.astype(jnp.bfloat16), ffn_in, preferred_element_type=jnp.fl...  47.9 us
  transfers between devices with their start and end apart: 6, of which 4 were waited for; matrix products, arithmetic and copies ran while one was open for 1% of the time, Pallas kernels for 0%

commit v1 on v0

v1 whole, which is shorter than its diff:
```python
import functools

import jax
import jax.numpy as jnp
from jax import lax
from jax.experimental import pallas as pl
from jax.experimental.pallas import tpu as pltpu
from jax.sharding import PartitionSpec as P

HEADS = 16
HDIM = 64
TASKS = 8
CLASSES = 3
SEGS = 8
LANES = 128
CHUNKS = 4
EPSILON = 1e-05
MOMENTUM = 0.9
AVERAGE = 0.8
RATE_D = 5.0
RATE_B = 20.0
RATE_HEADS = 0.3
NEG = -1e30
BF = jnp.bfloat16
F32 = jnp.float32
MESH = pl.DeviceIdType.MESH


def mm(left, right):
    return jnp.dot(left, right, preferred_element_type=F32)


def mm_t(left, right):
    return lax.dot_general(left, right, (((1,), (1,)), ((), ())), preferred_element_type=F32)


def mm_l(left, right):
    return lax.dot_general(left, right, (((0,), (0,)), ((), ())), preferred_element_type=F32)


def normed(values):
    centred = values - jnp.mean(values, -1, keepdims=True)
    rstd = lax.rsqrt(jnp.mean(centred * centred, -1, keepdims=True) + EPSILON)
    return centred * rstd, rstd


def norm_back(hat, rstd, gain, grad):
    scaled = grad * gain
    return rstd * (
        scaled
        - jnp.mean(scaled, -1, keepdims=True)
        - hat * jnp.mean(scaled * hat, -1, keepdims=True)
    )


def iota(shape, dim):
    return lax.broadcasted_iota(jnp.int32, shape, dim)


def update(weight, grad, moment, average, rate):
    moment_new = MOMENTUM * moment + grad
    weight_new = weight - rate * (grad + MOMENTUM * moment_new)
    return (moment_new, weight_new, AVERAGE * average + (1.0 - AVERAGE) * weight_new)


def step_kernel(
    cfg,
    fill, task_w, ids, seg, tasks, labels, places, gains, shifts, biases, bias_in, scale_d, scale_b, table,
    raw, qkv_h, out_h, fin_h, fout_h, va_h, vb_h,
    heads_sum, small_sum,
    x, qkv, outw, fin, fout, va, vb,
    lead_out, lead_in, seg_eff, starts_s, xz_s, latent_s, eq_s, qk, expo, ub, ua, ev, pack, rs_in,
    act, slope, gh, tab, gpack, g_in, zq, zacc, zb, gq_s, fx,
    cnt_out, cnt_in, hs, h_in, hr, hr_in, ag, late, lz_in, lr, lr_in,
    load_sem, x_sem, e1_s, e1_r, cnt_ss, cnt_rs, rs_s, rs_r, g_s, g_r, h_ss, h_rs, hr_ss, hr_rs, ag_ss, ag_rs,
    lz_ss, lz_rs, lr_ss, lr_rs,
):
    R, S, G, NR, V = cfg
    D = x.shape[1]
    FF = fin.shape[1]
    PAIRS = HEADS // 2
    L = R * SEGS
    z = lax.axis_index("heads")
    rw = lax.axis_index("rows")
    own_r = lax.rem(z, R)

    loads = [
        pltpu.make_async_copy(src, dst, load_sem.at[i])
        for i, (src, dst) in enumerate(
            ((va_h, va), (vb_h, vb), (qkv_h, qkv), (out_h, outw), (fin_h, fin), (fout_h, fout))
        )
    ]
    x_loads = [
        pltpu.make_async_copy(raw.at[pl.ds(r * S, S)], x.at[pl.ds(r * S, S)], x_sem.at[r]) for r in range(R)
    ]
    for copy in x_loads + loads:
        copy.start()

    barrier = pltpu.get_barrier_semaphore()
    for d in range(1, G):
        pl.semaphore_signal(barrier, inc=1, device_id={"heads": lax.rem(z + d, G)}, device_id_type=MESH)
    for d in range(1, NR):
        pl.semaphore_signal(barrier, inc=1, device_id={"rows": lax.rem(rw + d, NR)}, device_id_type=MESH)
    pl.semaphore_wait(barrier, G - 1 + NR - 1)

    def over(axis, d, src, dst, send, recv):
        me, size = (z, G) if axis == "heads" else (rw, NR)
        return pltpu.make_async_remote_copy(
            src_ref=src, dst_ref=dst, send_sem=send, recv_sem=recv,
            device_id={axis: lax.rem(me + d, size)}, device_id_type=MESH,
        )

    lane = iota((1, LANES), 1)
    low_half = lane < HDIM
    jcol = iota((SEGS, 1), 0)
    slot = iota((1, S), 1)

    def expand(f):
        tiles = [jnp.where(low_half, f[:, 2 * t : 2 * t + 1], f[:, 2 * t + 1 : 2 * t + 2]) for t in range(PAIRS)]
        return jnp.concatenate(tiles, 1)

    def compress(v):
        out = jnp.zeros((v.shape[0], LANES), F32)
        for t in range(PAIRS):
            tile = v[:, LANES * t : LANES * (t + 1)]
            a = jnp.sum(jnp.where(low_half, tile, 0.0), -1, keepdims=True)
            b = jnp.sum(jnp.where(low_half, 0.0, tile), -1, keepdims=True)
            out = jnp.where(lane == 2 * t, a, jnp.where(lane == 2 * t + 1, b, out))
        return out

    eye = iota((SEGS, SEGS), 0) == iota((SEGS, SEGS), 1)
    task_lane = lax.div(lane, CLASSES)
    counts = jnp.zeros((SEGS, LANES), F32)
    for r in range(R):
        seg_row = seg[r : r + 1, :]
        local = ids[r : r + 1, :] - z * V
        own = (local >= 0) & (local < V)
        first = (slot == 0) | (seg_row != pltpu.roll(seg_row, 1, 1))
        seg_eff[r : r + 1, :] = jnp.where(own & (first | (slot < fill[r])), seg_row, -1)
        pick = (seg_row == jcol) & first & own
        starts = jnp.sum((seg_row < jcol).astype(jnp.int32), 1, keepdims=True)
        starts_s[r] = jnp.broadcast_to(starts, (SEGS, LANES))
        lead = (starts < fill[r]).astype(F32)
        task = jnp.sum(jnp.where(eye, tasks[r : r + 1, :], 0), 1, keepdims=True)
        counts = counts + jnp.where((task == task_lane) & (lane < TASKS * CLASSES), lead, 0.0)
        x_loads[r].wait()
        fx[r * SEGS : (r + 1) * SEGS, :] = mm(pick.astype(F32).astype(BF), x[r * S : (r + 1) * S, :])
    lead_out[...] = fx[...].astype(BF)
    cnt_out[...] = counts
    e1 = [over("heads", d, lead_out, lead_in.at[d], e1_s.at[d], e1_r.at[d]) for d in range(1, G)]
    cnt = [over("rows", d, cnt_out, cnt_in.at[d], cnt_ss.at[d], cnt_rs.at[d]) for d in range(1, NR)]
    for copy in e1 + cnt:
        copy.start()

    gain0, shift0 = gains[0:1, :], shifts[0:1, :]
    prow = iota((places.shape[0], 1), 0)
    BLK = 256

    def norm_row(r, _):
        seg_row = seg[pl.ds(r, 1), :]
        begin = jnp.sum(jnp.where(seg_row == jcol, starts_s[r][:, 0:1], 0), 0, keepdims=True)
        offset = slot - begin
        for b in range(S // BLK):
            one = (prow == offset[:, b * BLK : (b + 1) * BLK]).astype(F32).astype(BF)
            rows = pl.ds(pl.multiple_of(r * S + b * BLK, BLK), BLK)
            hat, _ = normed(mm_l(one, places[...]) + x[rows, :].astype(F32))
            x[rows, :] = (hat * gain0 + shift0).astype(BF)
        return 0

    lax.fori_loop(0, R, norm_row, 0)

    for copy in e1:
        copy.wait()
    word = lead_out[...].astype(F32)
    for d in range(1, G):
        word = word + lead_in[d].astype(F32)
    hat, _ = normed(word + places[0:1, :].astype(F32))
    xz = hat * gain0 + shift0
    xz_s[...] = xz
    xl = xz.astype(BF)
    loads[0].wait()
    latent = mm(xl, va[...])
    latent_s[...] = latent
    loads[1].wait()
    eq_s[...] = mm((latent * scale_d[0:1, :]).astype(BF), vb[...])
    loads[2].wait()

    def tile_at(t):
        return pl.ds(pl.multiple_of(LANES * t, LANES), LANES)

    def absorb(t, _):
        r = mm(xl, qkv[:, pl.ds(pl.multiple_of(384 * t, LANES), 256)])
        at = tile_at(t)
        q = jnp.where(low_half, r[:, :LANES], r[:, LANES:]) + (biases[0:1, at] + scale_b[0:1, at] * eq_s[:, at])
        turned = pltpu.roll(q.astype(BF).astype(F32) * 0.125, HDIM, 1)
        a0 = mm_t(jnp.where(low_half, 0.0, turned).astype(BF), qkv[:, tile_at(3 * t)])
        a1 = mm_t(jnp.where(low_half, turned, 0.0).astype(BF), qkv[:, tile_at(3 * t + 2)])
        both = pl.ds(pl.multiple_of(16 * t, 16), 16)
        for r_ in range(R):
            rows = slice(r_ * SEGS, (r_ + 1) * SEGS)
            qk[r_, both, :] = jnp.concatenate([a0[rows], a1[rows]], 0).astype(BF)
        return 0

    lax.fori_loop(0, PAIRS, absorb, 0)

    Q = HEADS * SEGS
    qj = lax.rem(iota((Q, 1), 0), SEGS)
    hsub = iota((HEADS, SEGS, LANES), 0)
    hlane = iota((HEADS, SEGS, LANES), 2)

    def to_lanes(col):
        return jnp.sum(jnp.where(hsub == hlane, col.reshape(HEADS, SEGS, 1), 0.0), 0)

    def to_col(f):
        wide = jnp.broadcast_to(f[None], (HEADS, SEGS, LANES))
        return jnp.sum(jnp.where(hsub == hlane, wide, 0.0), -1, keepdims=True).reshape(Q, 1)

    def attend(p, _):
        parts = []
        for i in range(2):
            r = 2 * p + i
            xr = x[pl.ds(pl.multiple_of(r * S, S), S), :]
            mask = seg_eff[pl.ds(r, 1), :] == qj
            sc = jnp.where(mask, mm_t(qk[r], xr), NEG)
            top = jnp.max(sc, -1, keepdims=True)
            e = jnp.where(mask, jnp.exp(sc - top), 0.0)
            expo[r] = e
            pack[r, :, D : D + LANES] = to_lanes(top)
            pack[r, :, D + LANES :] = to_lanes(jnp.sum(e, -1, keepdims=True))
            parts.append(mm(e.astype(BF), xr).reshape(HEADS, SEGS, D))
        ub[:, pl.ds(pl.multiple_of(2 * SEGS * p, 2 * SEGS), 2 * SEGS), :] = jnp.concatenate(parts, 1).astype(BF)
        return 0

    lax.fori_loop(0, R // 2, attend, 0)

    NT = 256

    def cols(n):
        return pl.ds(pl.multiple_of(NT * n, NT), NT)

    def latents(n, _):
        ua[:, cols(n)] = mm(ub[...].reshape(HEADS * L, D), va[:, cols(n)])
        return 0

    lax.fori_loop(0, D // NT, latents, 0)

    def two(t):
        return pl.ds(pl.multiple_of(2 * L * t, 2 * L), 2 * L)

    def values(t, _):
        at = tile_at(t)
        v0 = mm(ub[2 * t], qkv[:, tile_at(3 * t + 1)])
        v1 = mm(ub[2 * t + 1], qkv[:, tile_at(3 * t + 2)])
        pair = mm((ua[two(t), :] * scale_d[1:2, :]).astype(BF), vb[:, at])
        extra = jnp.where(low_half, pair[:L], pair[L:])
        ev[:, at] = extra
        mixed = jnp.where(low_half, v0, v1) + scale_b[1:2, at] * extra
        pack[:, :, at] = mixed.reshape(R, SEGS, LANES)
        return 0

    lax.fori_loop(0, PAIRS, values, 0)

    rs = [
        over("heads", d, pack.at[lax.rem(lax.rem(z + d, G), R)], rs_in.at[d], rs_s.at[d], rs_r.at[d])
        for d in range(1, G)
    ]
    for copy in rs:
        copy.start()

    for copy in cnt:
        copy.wait()
    total = cnt_out[...]
    for d in range(1, NR):
        total = total + cnt_in[d]
    count = jnp.sum(total, 0, keepdims=True)
    weights = jnp.zeros((1, LANES), F32)
    for t in range(TASKS):
        weights = jnp.where(task_lane == t, task_w[t].astype(F32), weights)
    coef = weights / jnp.maximum(count, 1.0)
    task = jnp.sum(jnp.where(eye, tasks[pl.ds(own_r, 1), :], 0), 1, keepdims=True)
    label = jnp.sum(jnp.where(eye, labels[pl.ds(own_r, 1), :], 0), 1, keepdims=True)
    picked = (task == task_lane) & (lane < TASKS * CLASSES)
    target = picked & (lane - CLASSES * task_lane == label)
    leads = (starts_s[own_r][:, 0:1] < fill[own_r]) & (z < R)
    weight = jnp.sum(jnp.where(target, coef, 0.0), -1, keepdims=True)
    weight = jnp.where(leads, weight, 0.0)
    tab[...] = jnp.concatenate([table[...], jnp.zeros((LANES - TASKS * CLASSES, D), F32)], 0).astype(BF)

    for copy in rs:
        copy.wait()
    got = [pack[own_r]] + [rs_in[d] for d in range(1, G)]
    top = got[0][:, D : D + LANES]
    for part in got[1:]:
        top = jnp.maximum(top, part[:, D : D + LANES])
    shrink = [jnp.exp(part[:, D : D + LANES] - top) for part in got]
    tot = jnp.zeros((SEGS, LANES), F32)
    for part, s in zip(got, shrink):
        tot = tot + part[:, D + LANES :] * s
    tot = jnp.where(lane < HEADS, tot, 1.0)
    mixed = jnp.zeros((SEGS, D), F32)
    for part, s in zip(got, shrink):
        mixed = mixed + expand(s / tot) * part[:, :D]
    mixed = mixed + biases[1:2, :]
    gpack[:, D : D + LANES] = top + jnp.log(tot)

    loads[3].wait()
    r_one = xz_s[pl.ds(pl.multiple_of(own_r * SEGS, SEGS), SEGS), :] + mm(mixed.astype(BF), outw[...]) + biases[2:3, :]
    hat1, rstd1 = normed(r_one)
    x_one = hat1 * gains[1:2, :] + shifts[1:2, :]
    x_one_low = x_one.astype(BF)
    loads[4].wait()

    def hidden(n, _):
        at = cols(n)
        h = mm(x_one_low, fin[:, at]) + bias_in[:, at]
        half = 0.5 * (1.0 + lax.erf(h * 0.7071067811865476))
        act[:, at] = h * half
        slope[:, at] = half + h * (0.3989422804014327 * jnp.exp(-0.5 * h * h))
        return 0

    lax.fori_loop(0, FF // NT, hidden, 0)
    loads[5].wait()
    act_low = act[...].astype(BF)

    def ffn_out_tile(n, _):
        fx[0:SEGS, cols(n)] = mm(act_low, fout[:, cols(n)])
        return 0

    lax.fori_loop(0, D // NT, ffn_out_tile, 0)
    hat2, rstd2 = normed(x_one + fx[0:SEGS, :] + biases[3:4, :])
    x_two = (hat2 * gains[2:3, :] + shifts[2:3, :]).astype(BF)
    logits = mm_t(x_two, tab[...])
    chosen = jnp.where(picked, logits, NEG)
    peak = jnp.max(chosen, -1, keepdims=True)
    sums = jnp.sum(jnp.where(picked, jnp.exp(chosen - peak), 0.0), -1, keepdims=True)
    log_sum = peak + jnp.log(sums)
    hit = jnp.sum(jnp.where(target, logits, 0.0), -1, keepdims=True)
    loss = jnp.sum(weight * (log_sum - hit), 0, keepdims=True)
    soft = jnp.where(picked, jnp.exp(chosen - log_sum), 0.0) - target.astype(F32)
    g_logits = (weight * soft).astype(BF)
    hs[...] = mm(g_logits.astype(F32).T.astype(BF), x_two)[: CHUNKS * 8, :]
    hs[TASKS * CLASSES : TASKS * CLASSES + 8, :] = jnp.broadcast_to(loss, (8, D))
    g_two = mm(g_logits, tab[...])
    g_r2 = norm_back(hat2, rstd2, gains[2:3, :], g_two)
    g_f = g_r2.astype(BF)

    def back_hidden(n, _):
        at = cols(n)
        gh[:, at] = mm_t(g_f, fout[at, :]) * slope[:, at]
        return 0

    lax.fori_loop(0, FF // NT, back_hidden, 0)
    gh_low = gh[...].astype(BF)

    def back_in(n, _):
        fx[0:SEGS, cols(n)] = mm_t(gh_low, fin[cols(n), :])
        return 0

    lax.fori_loop(0, D // NT, back_in, 0)
    g_r1 = norm_back(hat1, rstd1, gains[1:2, :], g_r2 + fx[0:SEGS, :])
    g_mixed = mm_t(g_r1.astype(BF), outw[...]).astype(BF).astype(F32)
    gpack[:, 0:D] = g_mixed
    gpack[:, D + LANES :] = compress(g_mixed * mixed) - compress(g_mixed * biases[1:2, :])

    def spread(src, dst, send, recv, limit, action):
        for d in range(1, G):
            copy = over("heads", d, src(lax.rem(z + d, G)), dst(d), send.at[d], recv(d))
            cond = limit(lax.rem(z + d, G))
            if cond is None:
                action(copy)
            else:
                pl.when(cond)(functools.partial(action, copy))

    mine = None if G == R else z < R

    def g_from(r):
        return pltpu.make_async_remote_copy(
            src_ref=gpack, dst_ref=g_in.at[r], send_sem=g_s.at[0], recv_sem=g_r.at[r],
            device_id={"heads": z}, device_id_type=MESH,
        )

    spread(lambda _: gpack, lambda d: g_in.at[z] if G == R else g_in.at[own_r], g_s,
           lambda d: g_r.at[own_r], lambda peer: mine, lambda c: c.start())

    def chunk_of(peer):
        return hs.at[pl.ds(pl.multiple_of(8 * lax.rem(peer, CHUNKS), 8), 8)]

    def small(peer):
        return None if G == CHUNKS else peer < CHUNKS

    holder = None if G == CHUNKS else z < CHUNKS

    def guarded(cond, f):
        if cond is None:
            f()
        else:
            pl.when(cond)(f)

    spread(chunk_of, lambda d: h_in.at[d], h_ss, lambda d: h_rs.at[d], small, lambda c: c.start())

    def keep_own():
        g_in[own_r] = gpack[...]

    guarded(mine, keep_own)
    for r in range(R):
        pl.when(z != r)(lambda r=r: g_from(r).wait_recv())

    scale = [jnp.exp(pack[r, :, D : D + LANES] - g_in[r, :, D : D + LANES]) for r in range(R)]
    factor = jnp.concatenate([jnp.where(lane < HEADS, s, 0.0) for s in scale], 0)

    def back_value(t, acc):
        at = tile_at(t)
        g = g_in[:, :, at].reshape(L, LANES)
        z0 = mm_t(jnp.where(low_half, g, 0.0).astype(BF), qkv[:, tile_at(3 * t + 1)])
        z1 = mm_t(jnp.where(low_half, 0.0, g).astype(BF), qkv[:, tile_at(3 * t + 2)])
        zacc[two(t), :] = jnp.concatenate([z0, z1], 0)
        gb = g * scale_b[1:2, at]
        both = jnp.concatenate([jnp.where(low_half, gb, 0.0), jnp.where(low_half, 0.0, gb)], 0).astype(BF)
        back = mm_t(both, vb[:, at])
        f0 = jnp.sum(jnp.where(lane == 2 * t, factor, 0.0), -1, keepdims=True)
        f1 = jnp.sum(jnp.where(lane == 2 * t + 1, factor, 0.0), -1, keepdims=True)
        acc = acc + jnp.sum(jnp.concatenate([f0, f1], 0) * ua[two(t), :] * back, 0, keepdims=True)
        zb[two(t), :] = (back * scale_d[1:2, :]).astype(BF)
        return acc

    grad_d1 = lax.fori_loop(0, PAIRS, back_value, jnp.zeros((1, D), F32))
    grad_b1 = jnp.sum(g_in[:, :, 0:D].reshape(L, D) * ev[...] * expand(factor), 0, keepdims=True)

    def back_latent(n, _):
        at = cols(n)
        part = (zacc[:, at] + mm_t(zb[...], va[at, :])).reshape(HEADS, R, SEGS, NT)
        for r in range(R):
            zq[r, :, at] = part[:, r].reshape(Q, NT).astype(BF)
        return 0

    lax.fori_loop(0, D // NT, back_latent, 0)

    def relay():
        acc = chunk_of(z)[...]
        for d in range(1, G):
            over("heads", d, chunk_of(z), h_in.at[d], h_ss.at[d], h_rs.at[d]).wait_recv()
            acc = acc + h_in[d]
        hr[...] = acc
        for d in range(1, NR):
            over("rows", d, hr, hr_in.at[d], hr_ss.at[d], hr_rs.at[d]).start()

    guarded(holder, relay)

    def attend_back(p, _):
        parts = []
        for i in range(2):
            r = 2 * p + i
            xr = x[pl.ds(pl.multiple_of(r * S, S), S), :]
            f = to_col(jnp.where(lane < HEADS, jnp.exp(pack[r, :, D : D + LANES] - g_in[r, :, D : D + LANES]), 0.0))
            delta = to_col(g_in[r, :, D + LANES :])
            ds = (expo[r] * f) * (mm_t(zq[r], xr) - delta)
            parts.append(mm(ds.astype(BF), xr).reshape(HEADS, SEGS, D))
        ub[:, pl.ds(pl.multiple_of(2 * SEGS * p, 2 * SEGS), 2 * SEGS), :] = jnp.concatenate(parts, 1).astype(BF)
        return 0

    lax.fori_loop(0, R // 2, attend_back, 0)

    def relay_two():
        acc = hr[...]
        for d in range(1, NR):
            over("rows", d, hr, hr_in.at[d], hr_ss.at[d], hr_rs.at[d]).wait()
            acc = acc + hr_in[d]
        ag[lax.rem(z, CHUNKS)] = acc
        for d in range(1, G):
            c = lax.rem(z, CHUNKS)
            over("heads", d, ag.at[c], ag.at[c], ag_ss.at[d], ag_rs.at[c]).start()

    guarded(holder, relay_two)

    def back_query(t, _):
        at = tile_at(t)
        k0 = mm(ub[2 * t], qkv[:, tile_at(3 * t)])
        k1 = mm(ub[2 * t + 1], qkv[:, tile_at(3 * t + 2)])
        gq_s[:, at] = pltpu.roll(jnp.where(low_half, k1, k0), HDIM, 1) * 0.125
        return 0

    lax.fori_loop(0, PAIRS, back_query, 0)
    g_query = gq_s[...]
    grad_b0 = jnp.sum(g_query * eq_s[...], 0, keepdims=True)
    back = mm_t((g_query * scale_b[0:1, :]).astype(BF), vb[...])
    grad_d0 = jnp.sum(latent_s[...] * back, 0, keepdims=True)
    four = jnp.concatenate([grad_d0, grad_d1, grad_b0, grad_b1], 0)
    late[...] = jnp.concatenate([four[:, : D // 2], four[:, D // 2 :]], 0)
    leg = [over("heads", d, late, lz_in.at[d], lz_ss.at[d], lz_rs.at[d]) for d in range(1, G)]
    for copy in leg:
        copy.start()
    for copy in leg:
        copy.wait()
    acc = late[...]
    for d in range(1, G):
        acc = acc + lz_in[d]
    lr[...] = acc
    leg = [over("rows", d, lr, lr_in.at[d], lr_ss.at[d], lr_rs.at[d]) for d in range(1, NR)]
    for copy in leg:
        copy.start()

    for c in range(CHUNKS):
        def arrive(c=c):
            pltpu.make_async_remote_copy(
                src_ref=ag.at[c], dst_ref=ag.at[c], send_sem=ag_ss.at[0], recv_sem=ag_rs.at[c],
                device_id={"heads": z}, device_id_type=MESH,
            ).wait_recv()

        pl.when(z != c)(arrive)
    heads_sum[...] = ag[...].reshape(CHUNKS * 8, D)
    spread(lambda _: gpack, lambda d: g_in.at[own_r], g_s, lambda d: g_r.at[own_r], lambda peer: mine,
           lambda c: c.wait_send())
    spread(chunk_of, lambda d: h_in.at[d], h_ss, lambda d: h_rs.at[d], small, lambda c: c.wait_send())

    def sent():
        for d in range(1, G):
            c = lax.rem(z, CHUNKS)
            over("heads", d, ag.at[c], ag.at[c], ag_ss.at[d], ag_rs.at[c]).wait_send()

    guarded(holder, sent)
    for copy in leg:
        copy.wait()
    acc = lr[...]
    for d in range(1, NR):
        acc = acc + lr_in[d]
    small_sum[...] = acc


def on_device(
    sizes,
    token_ids, segment_ids, row_fill, task_ids, labels, task_weights,
    word_table, position_table, norm_gains, norm_biases, dense_biases,
    qkv_weight, out_weight, ffn_in, ffn_bias, ffn_out, vera_a, vera_b,
    scale_d, scale_b, task_heads, mom_d, mom_b, mom_heads, avg_d, avg_b, avg_heads,
):
    G, NR = sizes
    R, S = token_ids.shape
    V, D = word_table.shape
    FF = ffn_in.shape[1]
    L, Q, T = R * SEGS, HEADS * SEGS, R * S
    WIDE = D + 2 * LANES
    z = lax.axis_index("heads")
    local = jnp.clip(token_ids.reshape(-1) - z * V, 0, V - 1)
    raw = jnp.take(word_table, local, axis=0)
    table = task_heads.reshape(TASKS * CLASSES, D)
    v = pltpu.VMEM
    dma = pltpu.SemaphoreType.DMA
    scratch = [
        v((T, D), BF), v(qkv_weight.shape, BF), v(out_weight.shape, BF), v(ffn_in.shape, BF), v(ffn_out.shape, BF),
        v(vera_a.shape, BF), v(vera_b.shape, BF),
        v((L, D), BF), v((G, L, D), BF), v((R, S), jnp.int32), v((R, SEGS, LANES), jnp.int32), v((L, D), F32),
        v((L, D), F32), v((L, D), F32), v((R, Q, D), BF), v((R, Q, S), F32), v((HEADS, L, D), BF),
        v((HEADS * L, D), F32), v((L, D), F32), v((R, SEGS, WIDE), F32), v((G, SEGS, WIDE), F32),
        v((SEGS, FF), F32), v((SEGS, FF), F32), v((SEGS, FF), F32), v((LANES, D), BF), v((SEGS, WIDE), F32),
        v((R, SEGS, WIDE), F32), v((R, Q, D), BF), v((HEADS * L, D), F32), v((HEADS * L, D), BF), v((L, D), F32),
        v((L, D), F32),
        v((SEGS, LANES), F32), v((NR, SEGS, LANES), F32), v((CHUNKS * 8, D), F32), v((G, 8, D), F32), v((8, D), F32),
        v((NR, 8, D), F32), v((CHUNKS, 8, D), F32), v((8, D // 2), F32), v((G, 8, D // 2), F32), v((8, D // 2), F32),
        v((NR, 8, D // 2), F32),
        dma((6,)), dma((R,)), dma((G,)), dma((G,)), dma((NR,)), dma((NR,)), dma((G,)), dma((G,)),
        dma((G,)), dma((R,)), dma((G,)), dma((G,)), dma((NR,)), dma((NR,)), dma((G,)), dma((CHUNKS,)),
        dma((G,)), dma((G,)), dma((NR,)), dma((NR,)),
    ]
    vm, hbm, sm = (pl.BlockSpec(memory_space=m) for m in (pltpu.VMEM, pl.ANY, pltpu.SMEM))
    heads_sum, small_sum = pl.pallas_call(
        functools.partial(step_kernel, (R, S, G, NR, V)),
        out_shape=(jax.ShapeDtypeStruct((CHUNKS * 8, D), F32), jax.ShapeDtypeStruct((8, D // 2), F32)),
        in_specs=[sm, sm] + [vm] * 12 + [hbm] * 7,
        out_specs=(vm, vm),
        scratch_shapes=scratch,
        compiler_params=pltpu.CompilerParams(
            collective_id=0, has_side_effects=True, vmem_limit_bytes=60 * 1024 * 1024
        ),
    )(
        row_fill, task_weights, token_ids, segment_ids, task_ids, labels, position_table[2:], norm_gains, norm_biases,
        dense_biases, ffn_bias.reshape(1, -1), scale_d, scale_b, table,
        raw, qkv_weight, out_weight, ffn_in, ffn_out, vera_a, vera_b,
    )
    four = jnp.concatenate([small_sum[:4], small_sum[4:]], 1)
    grad_d, grad_b = four[:2], four[2:]
    grad_heads = heads_sum[: TASKS * CLASSES].reshape(TASKS, CLASSES, D)
    loss = heads_sum[TASKS * CLASSES, 0]
    m_d, w_d, a_d = update(scale_d, grad_d, mom_d, avg_d, RATE_D)
    m_b, w_b, a_b = update(scale_b, grad_b, mom_b, avg_b, RATE_B)
    m_h, w_h, a_h = update(task_heads, grad_heads, mom_heads, avg_heads, RATE_HEADS)
    stats = jnp.stack([jnp.sqrt(jnp.mean(w_d * w_d)), jnp.sqrt(jnp.mean(w_b * w_b))])
    return (loss, m_d, m_b, m_h, w_d, w_b, w_h, a_d, a_b, a_h, w_h.astype(BF), stats)


def solution(mesh):
    sizes = (mesh.shape["heads"], mesh.shape["rows"])
    by_row = P("rows", None)
    return jax.shard_map(
        functools.partial(on_device, sizes),
        mesh=mesh,
        in_specs=(by_row, by_row, P("rows"), by_row, by_row, P(), P("heads", None)) + (P(),) * 20,
        out_specs=(P(),) * 12,
        check_vma=False,
    )
```

time: 1510 us -> 142 us (0.09)
  waiting for transfers between devices: 796 us -> 0 us
  matrix products: 377 us -> 0 us
  blocking collectives: 110 us -> 0 us
  Pallas kernels: 0 us -> 88.5 us
  other arithmetic: 90.1 us -> 11.9 us
  local copies, waits for them, and re-layouts: 103 us -> 39.4 us
    all_gather x1 -> x0, waiting for transfers between devices: 425 us -> none  [on_device(): pieces = lax.all_gather(packed_in, 'heads', axis=0, tiled=True)]
    dot_general x41 -> x0, matrix products: 377 us -> none  [the longest x8 62.8 us: row_scores(): jnp.einsum('qhe,khe->hqk', query, key, preferred_element_type=jnp.float32)]
    psum x1 -> x0, waiting for transfers between devices: 185 us -> none  [on_device(): lax.psum((grad_d, grad_b, grad_heads, loss_part), ('rows', 'heads'))]
    reduce_scatter x1 -> x0, waiting for transfers between devices: 138 us -> none  [on_device(): lax.psum_scatter(jnp.where(inside[:, None], found, 0.0).astype(jnp.bfloat...]
    psum x2 -> x0, blocking collectives: 110 us -> none  [the longest x1 68.1 us: on_device(): lax.psum(jnp.sum(pick * leading[:, None].astype(jnp.float32), 0), ('rows'...]
    pallas_call x0 -> x1, Pallas kernels: none -> 88.5 us  [on_device(): pl.pallas_call(functools.partial(step_kernel, (R, S, G, NR, V)), out_shap...]
    all_to_all x3 -> x0, waiting for transfers between devices: 47.7 us -> none  [the longest x1 47.7 us: on_device(): lax.all_to_all(grad_mixed, 'heads', split_axis=1, concat_axis=0, tiled=True)]
    reduce_sum x17 -> x0, other arithmetic: 31.8 us -> none  [the longest x4 14.6 us: attend(): total = jnp.sum(expo, -1, keepdims=True)]
  transfers between devices with their start and end apart: 6 -> 0, of which waited for: 4 -> 0; matrix products, arithmetic and copies ran while one was open for 1% -> 0% of each run, Pallas kernels for 0% -> 0%
where the time goes in v1:
time: 142 us
  Pallas kernels  88.5 us (62%)
  local copies, waits for them, and re-layouts  39.4 us (28%)
  other arithmetic  11.9 us (8%)
  between operations  2.17 us (2%)
    pallas_call x1, Pallas kernels, on_device(): pl.pallas_call(functools.partial(step_kernel, (R, S, G, NR, V)), out_shap...  88.5 us
    gather x1, local copies, waits for them, and re-layouts, on_device(): raw = jnp.take(word_table, local, axis=0)  32.7 us
    select_n x2, other arithmetic, on_device(): raw = jnp.take(word_table, local, axis=0)  7.31 us

profile of v1, /device:TPU:0, one launch (start us, length us, event | category | flops | bytes accessed | tf_op | source)
XLA Modules:
  0.0 141.9 jit_solution(17833260254963097930)
XLA Ops:
  0.6 0.7 fusion.1
  1.5 1.0 copy.50
  2.4 0.7 reshape.73.table
  3.1 2.0 %slice.21.places = bf16[256,1024]{1,0:T(8,128)(2,1)} slice(bf16[258,1024]{1,0:T(8,128)(2,1)} %param.34), slice={[2:258], [0:1024]} | slice | bytes 1048576 | tf_op jit(solution)/shard_map/slice | solution.py:575
  5.1 32.7 %gather_fusion = bf16[4096,1024]{1,0:T(8,128)(2,1)} fusion(bf16[12568,1024]{1,0:T(8,128)(2,1)} %param.33, s32[4096]{0:T(1024)S(1)} %broadcast_clamp_fusion), kind=kCustom, calls=%fused_computation | custom fusion | bytes 16793600 | tf_op jit(solution)/shard_map/jit(_take)/gather | solution.py:544
  37.8 7.3 %broadcast_select_fusion.raw = bf16[4096,1024]{1,0:T(8,128)(2,1)} fusion(bf16[4096,1024]{1,0:T(8,128)(2,1)} %gather_fusion, pred[4096]{0:T(1024)(128)(4,1)S(1)} %compare_and_fusion), kind=kLoop, calls=%fused_computation.1 | loop fusion | flops 4194304 | bytes 16781312 | tf_op jit(solution)/shard_map/jit(_take)/select_n | solution.py:544
  45.1 0.0 copy-start.8
  45.1 0.0 copy-start.9
  45.1 0.0 copy-start
  45.2 0.0 copy-start.2
  45.2 0.0 copy-start.3
  45.2 88.5 %shard_map.346 = (f32[32,1024]{1,0:T(8,128)}, f32[8,512]{1,0:T(8,128)}) custom-call(s32[4]{0:T(128)} %fill.1, s32[8]{0:T(128)} %task_w.1, s32[4,1024]{1,0:T(4,128)} %ids.1, s32[4,1024]{1,0:T(4,128)} %seg.1, s32[4,8]{1,0:T(4,128)} %tasks.1, s32[4,8]{1,0:T(4,128)} %labels.1, bf16[256,1024]{1,0:T(8,128)(2,1)} %slice.21.places, f32[3,1024]{1,0:T(4,128)} %gains.1, ...), custom_call_target="tpu_custom_call" | custom-call | tf_op jit(solution)/shard_map/pallas_call | solution.py:565
  133.7 1.2 slice.22
  134.9 0.8 fusion.4
  135.7 0.0 copy-done.6
  135.7 0.0 copy-done.7
  135.7 0.0 copy-done.10
  135.7 0.0 copy-done.11
  135.7 1.2 multiply_reduce_fusion
  138.4 0.6 pad_maximum_fusion.1
  138.9 0.0 copy-done.8
  138.9 0.0 copy-done.9
  138.9 0.6 multiply_add_fusion.2
  139.6 0.9 slice.27
  140.5 0.0 copy-done
  140.5 0.0 copy-done.2
  140.5 0.7 fusion.3
  141.3 0.0 copy-done.3
  141.3 0.7 multiply_add_fusion
  141.9 0.0 copy-done.4
  141.9 0.0 copy-done.5
  141.9 0.0 copy-done.1
  (12 shorter events, 0.1 us)
Async XLA Ops:
  45.1 90.6 %copy-start.6 = (f32[2,1024]{1,0:T(2,128)S(1)}, f32[2,1024]{1,0:T(2,128)}, u32[]{:S(2)}) copy-start(f32[2,1024]{1,0:T(2,128)} %scale_d.1) | copy-start | bytes 24580
  45.1 90.6 %copy-start.7 = (f32[2,1024]{1,0:T(2,128)S(1)}, f32[2,1024]{1,0:T(2,128)}, u32[]{:S(2)}) copy-start(f32[2,1024]{1,0:T(2,128)} %scale_b.1) | copy-start | bytes 24580
  45.1 90.6 %copy-start.10 = (f32[2,1024]{1,0:T(2,128)S(1)}, f32[2,1024]{1,0:T(2,128)}, u32[]{:S(2)}) copy-start(f32[2,1024]{1,0:T(2,128)} %param.49) | copy-start | bytes 24580
  45.1 90.6 %copy-start.11 = (f32[2,1024]{1,0:T(2,128)S(1)}, f32[2,1024]{1,0:T(2,128)}, u32[]{:S(2)}) copy-start(f32[2,1024]{1,0:T(2,128)} %param.48) | copy-start | bytes 24580
  45.1 93.8 %copy-start.8 = (f32[2,1024]{1,0:T(2,128)S(1)}, f32[2,1024]{1,0:T(2,128)}, u32[]{:S(2)}) copy-start(f32[2,1024]{1,0:T(2,128)} %param.52) | copy-start | bytes 24580
  45.1 93.8 %copy-start.9 = (f32[2,1024]{1,0:T(2,128)S(1)}, f32[2,1024]{1,0:T(2,128)}, u32[]{:S(2)}) copy-start(f32[2,1024]{1,0:T(2,128)} %param.51) | copy-start | bytes 24580
  45.1 95.4 %copy-start = (f32[8,3,1024]{2,0,1:T(8,128)S(1)}, f32[8,3,1024]{2,0,1:T(8,128)}, u32[]{:S(2)}) copy-start(f32[8,3,1024]{2,0,1:T(8,128)} %param.47) | copy-start | bytes 294916
  45.2 95.4 %copy-start.2 = (f32[8,3,1024]{2,0,1:T(8,128)S(1)}, f32[8,3,1024]{2,0,1:T(8,128)}, u32[]{:S(2)}) copy-start(f32[8,3,1024]{2,0,1:T(8,128)} %param.50) | copy-start | bytes 294916
  45.2 96.1 %copy-start.3 = (f32[8,3,1024]{2,0,1:T(8,128)S(1)}, f32[8,3,1024]{2,0,1:T(8,128)}, u32[]{:S(2)}) copy-start(f32[8,3,1024]{2,0,1:T(8,128)} %param.53) | copy-start | bytes 294916
  137.0 5.0 %copy-start.4 = (f32[2,1024]{1,0:T(2,128)}, f32[2,1024]{1,0:T(2,128)S(1)}, u32[]{:S(2)}) copy-start(f32[2,1024]{1,0:T(2,128)S(1)} %get-tuple-element.32) | copy-start | bytes 24580
  137.0 5.0 %copy-start.5 = (f32[2,1024]{1,0:T(2,128)}, f32[2,1024]{1,0:T(2,128)S(1)}, u32[]{:S(2)}) copy-start(f32[2,1024]{1,0:T(2,128)S(1)} %get-tuple-element.38) | copy-start | bytes 24580
  141.3 0.7 copy-start.1
